TPU v7x, 32 devices: a whole 2x2x4 slice. The times are simulated.
32 devices in a mesh: row: 4 (over y, x), col: 8 (over z, core).
Axes of the slice: x: 2, y: 2, z: 4, core: 2. Of those that a mesh axis runs over, the one named last changes fastest.
Arguments:
- features: bfloat16 [128, 1024, 256], P('row', 'col'), may hold values from -6 to 6
- conv_weight: bfloat16 [3, 3, 3, 256, 256], replicated, may hold values from -0.1875 to 0.1875
- conv_bias: float32 [3, 256], replicated, may hold values from -3 to 3
- boxes: int32 [4, 4, 8, 512], P(None, 'row', 'col'), may hold values from 0 to 256, as said below
- shards: int32 [4, 8, 512, 1], P('row', 'col'), may hold values from 0 to 31; in each aligned block of 512 rows (0 to 511, 512 to 1023, ..., all dimensions but the last counted through in order) at most 32 rows name the same one
- white_mean: float32 [256], replicated, may hold values from 0.2 to 1.5
- white_weight: bfloat16 [256, 1024], replicated, may hold values from -0.375 to 0.375
Outputs:
- index_rows: bfloat16 [32768, 1024], P(('row', 'col'))
Inputs may be any that keep to these rules, and one draw needn't show every extreme that they name: Region k of the device at row index i and column index j has j * 32 <= boxes[2, i, j, k] < (j + 1) * 32; boxes[0] < boxes[1] <= 32, boxes[2] < boxes[3] <= 256, and boxes[3] - boxes[2] <= 32. `shards`: at most 32 regions of one device share a shard.
All inputs are finite; a program needn't handle non-finite values.
Results may differ from a plain program's by a relative error of at most 0.009.
Values may be sent and summed in bfloat16 or wider, within the bound.
A program may use at most 128 MiB of HBM per device.

v0:
```python
import functools

import jax
import jax.numpy as jnp
from jax import lax
from jax.experimental import pallas as pl
from jax.experimental.pallas import tpu as pltpu
from jax.sharding import PartitionSpec as P

BLK = 4
EPSILON = 1e-06
PAD = 16
MESH = pl.DeviceIdType.MESH


def conv_kernel(n_row, n_col, feat, w, b, wide, a0, xa, xb, xc, load_sem, hs, hr, ms, mr):
    rows, cols, ch = feat.shape
    layers = w.shape[0]
    halo = layers
    wide_w = cols + 2 * PAD
    mid_w = xa.shape[1]
    brows = rows // BLK
    bcols = cols // BLK
    i = lax.axis_index("row")
    j = lax.axis_index("col")

    load = pltpu.make_async_copy(feat, a0.at[pl.ds(halo, rows), pl.ds(PAD, cols)], load_sem)
    load.start()

    barrier = pltpu.get_barrier_semaphore()
    for r in range(n_row):
        @pl.when(r != i)
        def _():
            pl.semaphore_signal(barrier, inc=1, device_id=(r, j), device_id_type=MESH)

        @pl.when(j > 0)
        def _():
            pl.semaphore_signal(barrier, inc=1, device_id=(r, jnp.maximum(j - 1, 0)), device_id_type=MESH)

        @pl.when(j < n_col - 1)
        def _():
            pl.semaphore_signal(barrier, inc=1, device_id=(r, jnp.minimum(j + 1, n_col - 1)), device_id_type=MESH)
    sides = jnp.where(j > 0, 1, 0) + jnp.where(j < n_col - 1, 1, 0)
    pl.semaphore_wait(barrier, n_row - 1 + n_row * sides)

    mid = pl.ds(halo, rows)
    to_left = pltpu.make_async_remote_copy(
        src_ref=feat.at[:, pl.ds(0, PAD)], dst_ref=a0.at[mid, pl.ds(PAD + cols, PAD)],
        send_sem=hs.at[0], recv_sem=hr.at[0],
        device_id=(i, jnp.maximum(j - 1, 0)), device_id_type=MESH)
    to_right = pltpu.make_async_remote_copy(
        src_ref=feat.at[:, pl.ds(cols - PAD, PAD)], dst_ref=a0.at[mid, pl.ds(0, PAD)],
        send_sem=hs.at[1], recv_sem=hr.at[1],
        device_id=(i, jnp.minimum(j + 1, n_col - 1)), device_id_type=MESH)
    to_up = pltpu.make_async_remote_copy(
        src_ref=a0.at[pl.ds(halo, halo)], dst_ref=a0.at[pl.ds(halo + rows, halo)],
        send_sem=hs.at[2], recv_sem=hr.at[2],
        device_id=(jnp.maximum(i - 1, 0), j), device_id_type=MESH)
    to_down = pltpu.make_async_remote_copy(
        src_ref=a0.at[pl.ds(rows, halo)], dst_ref=a0.at[pl.ds(0, halo)],
        send_sem=hs.at[3], recv_sem=hr.at[3],
        device_id=(jnp.minimum(i + 1, n_row - 1), j), device_id_type=MESH)

    @pl.when(j > 0)
    def _():
        to_left.start()

    @pl.when(j < n_col - 1)
    def _():
        to_right.start()

    @pl.when(j == 0)
    def _():
        a0[mid, 0:PAD, :] = jnp.zeros((rows, PAD, ch), a0.dtype)

    @pl.when(j == n_col - 1)
    def _():
        a0[mid, PAD + cols:wide_w, :] = jnp.zeros((rows, PAD, ch), a0.dtype)
        wide[:, bcols:2 * bcols, :] = jnp.zeros((wide.shape[0], bcols, ch), wide.dtype)

    @pl.when(i == 0)
    def _():
        a0[0:halo] = jnp.zeros((halo, wide_w, ch), a0.dtype)

    @pl.when(i == n_row - 1)
    def _():
        a0[halo + rows:2 * halo + rows] = jnp.zeros((halo, wide_w, ch), a0.dtype)

    load.wait()

    @pl.when(j < n_col - 1)
    def _():
        to_left.wait_recv()
        to_right.wait_send()

    @pl.when(j > 0)
    def _():
        to_right.wait_recv()
        to_left.wait_send()

    @pl.when(i > 0)
    def _():
        to_up.start()

    @pl.when(i < n_row - 1)
    def _():
        to_down.start()

    def spread(r):
        x = a0[r].astype(jnp.float32)
        for q in range(3):
            moved = pltpu.roll(x, wide_w - (PAD - halo) - q, 0)
            xa[r, :, q * ch:(q + 1) * ch] = moved[:mid_w].astype(xa.dtype)

    def taps(src, layer, r, count, width):
        acc = None
        for p in range(3):
            part = src[pl.ds(r + p, count), 0:width, :].reshape(count * width, 3 * ch)
            prod = jnp.dot(part, w[layer, p], preferred_element_type=jnp.float32)
            acc = prod if acc is None else acc + prod
        return jnp.maximum(acc + b[layer], 0.0)

    def inner(src, dst, layer, r, count, margin):
        y = taps(src, layer, r, count, mid_w)
        flat = lax.broadcasted_iota(jnp.int32, (count * mid_w, 1), 0)
        line = flat // mid_w
        row_at = r - margin + line
        col_at = flat - line * mid_w - margin
        ok = ((row_at >= 0) | (i > 0)) & ((row_at < rows) | (i < n_row - 1))
        ok = ok & ((col_at >= 0) | (j > 0)) & ((col_at < cols) | (j < n_col - 1))
        y = jnp.where(ok, y, 0.0)
        for q in range(3):
            moved = y if q == 0 else pltpu.roll(y, count * mid_w - q, 0)
            moved = moved.astype(dst.dtype).reshape(count, mid_w, ch)
            dst[pl.ds(r, count), :, q * ch:(q + 1) * ch] = moved[:, :dst.shape[1]]

    @pl.loop(halo, halo + rows)
    def _(r):
        spread(r)

    first = halo
    count1 = 3
    steps1 = (rows - 2) // count1

    @pl.loop(0, steps1)
    def _(s):
        inner(xa, xb, 0, first + s * count1, count1, 2)

    @pl.when(i < n_row - 1)
    def _():
        to_up.wait_recv()
        to_down.wait_send()

    @pl.when(i > 0)
    def _():
        to_down.wait_recv()
        to_up.wait_send()

    @pl.loop(0, halo)
    def _(r):
        spread(r)
        spread(r + halo + rows)

    @pl.loop(0, 2)
    def _(s):
        inner(xa, xb, 0, s * (rows + 1), count1, 2)

    @pl.loop(0, (rows + 2) // 4)
    def _(s):
        inner(xb, xc, 1, s * 4, 4, 1)

    inner(xb, xc, 1, rows, 2, 1)

    def move(bi, g, r):
        return pltpu.make_async_remote_copy(
            src_ref=wide.at[i * brows + bi, pl.ds(0, bcols)],
            dst_ref=wide.at[i * brows + bi, pl.ds(g * bcols, bcols)],
            send_sem=ms.at[bi, g * n_row + r], recv_sem=mr.at[bi, g * n_row + i],
            device_id=(r, j if g == 0 else jnp.maximum(j - 1, 0)), device_id_type=MESH)

    def arrive(bi, g, r):
        return pltpu.make_async_remote_copy(
            src_ref=wide.at[r * brows + bi, pl.ds(0, bcols)],
            dst_ref=wide.at[r * brows + bi, pl.ds(g * bcols, bcols)],
            send_sem=ms.at[bi, g * n_row + r], recv_sem=mr.at[bi, g * n_row + r],
            device_id=(r, j), device_id_type=MESH)

    @pl.loop(0, brows)
    def _(bi):
        y = taps(xc, 2, bi * BLK, BLK, cols)
        y = y.reshape(BLK, cols, ch)
        y = jnp.maximum(jnp.maximum(y[0], y[1]), jnp.maximum(y[2], y[3]))
        y = jnp.max(y.reshape(bcols, BLK, ch), axis=1)
        wide[i * brows + bi, 0:bcols, :] = y.astype(wide.dtype)
        for r in range(n_row):
            @pl.when(r != i)
            def _():
                move(bi, 0, r).start()

            @pl.when(j > 0)
            def _():
                move(bi, 1, r).start()

    @pl.loop(0, brows)
    def _(bi):
        for r in range(n_row):
            @pl.when(r != i)
            def _():
                move(bi, 0, r).wait_send()
                arrive(bi, 0, r).wait_recv()

            @pl.when(j > 0)
            def _():
                move(bi, 1, r).wait_send()

            @pl.when(j < n_col - 1)
            def _():
                arrive(bi, 1, r).wait_recv()


def pool_kernel(devices, capacity, boxes, shards, wide, out, table, part, lut):
    nrow, ncol2, ch = wide.shape
    halves = ch // 128
    regions = shards.shape[1]
    bcols = ncol2 // 2
    level_size = nrow * ncol2
    levels = table.shape[1] // level_size
    col_base = lax.axis_index("col") * bcols

    level = 0
    for size in range(1, nrow + 1):
        while 2 ** (level + 1) <= size:
            level += 1
        lut[0, size] = level * level_size
        lut[1, size] = level * level_size - (2 ** level) * ncol2

    @pl.loop(0, nrow)
    def _(r):
        x = wide[r].astype(jnp.float32)
        for h in range(halves):
            table[h, pl.ds(pl.multiple_of(r * ncol2, 8), ncol2), :] = x[:, h * 128:(h + 1) * 128]

    for lv in range(1, levels):
        step = 2 ** (lv - 1)
        below = (lv - 1) * level_size
        count = nrow - 2 ** lv + 1

        @pl.loop(0, count)
        def _(r):
            for h in range(halves):
                one = table[h, pl.ds(pl.multiple_of(below + r * ncol2, 8), ncol2), :]
                two = table[h, pl.ds(pl.multiple_of(below + (r + step) * ncol2, 8), ncol2), :]
                table[h, pl.ds(pl.multiple_of(below + level_size + r * ncol2, 8), ncol2), :] = (
                    jnp.maximum(one, two))

    sub = lax.broadcasted_iota(jnp.int32, (8, 128), 0)

    def pool(n):
        r0, r1, c0, c1 = (boxes[k, n] for k in range(4))
        span = jnp.maximum(r1 - r0, 1)
        c0 = jnp.maximum(c0 - col_base, 0)
        c1 = c1 - col_base
        high = lut[0, span] + r0 * ncol2
        low = jnp.maximum(lut[1, span] + r1 * ncol2, 0)
        last = jnp.maximum(c1 - 8, c0)
        starts = [c0, jnp.minimum(c0 + 8, last), jnp.minimum(c0 + 16, last), last]
        inside = sub < c1 - c0
        for h in range(halves):
            got = [table[h, pl.ds(base + c, 8), :] for base in (high, low) for c in starts]
            while len(got) > 1:
                got = [jnp.maximum(got[k], got[k + 1]) for k in range(0, len(got), 2)]
            part[h, pl.ds(pl.multiple_of(n * 8, 8), 8), :] = jnp.where(inside, got[0], 0.0)

    @pl.loop(0, regions // 4)
    def _(g):
        for k in range(4):
            pool(g * 4 + k)

    pooled = jnp.concatenate(
        [
            functools.reduce(
                jnp.maximum, [part[h, pl.ds(s, regions, stride=8), :] for s in range(8)])
            for h in range(halves)
        ],
        axis=1,
    ).astype(jnp.bfloat16)

    ids = shards[...]
    same = (lax.broadcasted_iota(jnp.int32, (devices, regions), 0) == ids).astype(jnp.float32)
    early = (lax.broadcasted_iota(jnp.int32, (regions, regions), 0)
             < lax.broadcasted_iota(jnp.int32, (regions, regions), 1)).astype(jnp.float32)
    before = jnp.dot(same.astype(jnp.bfloat16), early.astype(jnp.bfloat16),
                     preferred_element_type=jnp.float32)
    slot = jnp.sum(before * same, axis=0, keepdims=True)
    target = ids * capacity + slot.astype(jnp.int32)
    size = 256
    for s in range(devices * capacity // size):
        place = lax.broadcasted_iota(jnp.int32, (size, regions), 0) + s * size
        pick = (place == target).astype(jnp.float32)
        filled = jnp.sum(pick, axis=1, keepdims=True)
        moved = jnp.dot(pick.astype(jnp.bfloat16), pooled, preferred_element_type=jnp.float32)
        out[s * size:(s + 1) * size, :] = (moved + (filled - 1.0)).astype(out.dtype)


def scatter_kernel(n_row, n_col, src, dst, send_sem, recv_sem, own_sem):
    devices = n_row * n_col
    i = lax.axis_index("row")
    j = lax.axis_index("col")
    me = i * n_col + j
    own = pltpu.make_async_copy(src.at[me], dst.at[me], own_sem)
    own.start()
    barrier = pltpu.get_barrier_semaphore()

    @pl.loop(1, devices)
    def _(k):
        to = lax.rem(me + k, devices)
        pl.semaphore_signal(barrier, inc=1, device_id=(to // n_col, lax.rem(to, n_col)),
                            device_id_type=MESH)

    pl.semaphore_wait(barrier, devices - 1)

    def copy(k):
        to = lax.rem(me + k, devices)
        return pltpu.make_async_remote_copy(
            src_ref=src.at[to], dst_ref=dst.at[me],
            send_sem=send_sem.at[k], recv_sem=recv_sem.at[k],
            device_id=(to // n_col, lax.rem(to, n_col)), device_id_type=MESH)

    def got(k):
        away = lax.rem(me + devices - k, devices)
        return pltpu.make_async_remote_copy(
            src_ref=src.at[away], dst_ref=dst.at[away],
            send_sem=send_sem.at[k], recv_sem=recv_sem.at[k],
            device_id=(away // n_col, lax.rem(away, n_col)), device_id_type=MESH)

    @pl.loop(1, devices)
    def _(k):
        copy(k).start()

    own.wait()

    @pl.loop(1, devices)
    def _(k):
        copy(k).wait_send()
        got(k).wait_recv()


def describe_kernel(got, mean, weight, out):
    values = got[...].astype(jnp.float32)
    scale = lax.rsqrt(jnp.mean(values * values, axis=-1, keepdims=True) + EPSILON)
    centered = (values * scale - mean[...]).astype(jnp.bfloat16)
    white = jnp.dot(centered, weight[...], preferred_element_type=jnp.float32)
    scale = lax.rsqrt(jnp.mean(white * white, axis=-1, keepdims=True) + EPSILON)
    filled = values[:, 0:1] >= 0.0
    out[...] = jnp.where(filled, white * scale, 0.0).astype(out.dtype)


def body(n_row, n_col, features, conv_weight, conv_bias, boxes, shards, white_mean, white_weight):
    rows, cols, ch = features.shape
    layers = conv_weight.shape[0]
    devices = n_row * n_col
    regions = boxes.shape[-1]
    capacity = max(2, 2 * regions // devices)
    brows, bcols = rows // BLK, cols // BLK
    mid_w = cols + 16
    vmem = pl.BlockSpec(memory_space=pltpu.VMEM)
    any_spec = pl.BlockSpec(memory_space=pl.ANY)
    bf16 = jnp.bfloat16
    wide = pl.pallas_call(
        functools.partial(conv_kernel, n_row, n_col),
        out_shape=jax.ShapeDtypeStruct((n_row * brows, 2 * bcols, ch), bf16),
        in_specs=[any_spec, vmem, vmem],
        out_specs=vmem,
        scratch_shapes=[
            pltpu.VMEM((rows + 2 * layers, cols + 2 * PAD, ch), bf16),
            pltpu.VMEM((rows + 6, mid_w, 3 * ch), bf16),
            pltpu.VMEM((rows + 4, mid_w, 3 * ch), bf16),
            pltpu.VMEM((rows + 2, cols, 3 * ch), bf16),
            pltpu.SemaphoreType.DMA,
            pltpu.SemaphoreType.DMA((4,)),
            pltpu.SemaphoreType.DMA((4,)),
            pltpu.SemaphoreType.DMA((brows, 2 * n_row)),
            pltpu.SemaphoreType.DMA((brows, 2 * n_row)),
        ],
        compiler_params=pltpu.CompilerParams(
            collective_id=0, has_side_effects=True, vmem_limit_bytes=56 * 2**20),
    )(features, conv_weight.reshape(layers, 3, 3 * ch, ch), conv_bias.reshape(layers, 1, ch))

    nbr = n_row * brows
    levels = nbr.bit_length()
    outgoing = pl.pallas_call(
        functools.partial(pool_kernel, devices, capacity),
        out_shape=jax.ShapeDtypeStruct((devices * capacity, ch), bf16),
        in_specs=[pl.BlockSpec(memory_space=pltpu.SMEM), vmem, vmem],
        out_specs=vmem,
        scratch_shapes=[
            pltpu.VMEM((ch // 128, levels * nbr * 2 * bcols, 128), jnp.float32),
            pltpu.VMEM((ch // 128, regions * 8 + 8, 128), jnp.float32),
            pltpu.SMEM((2, nbr + 1), jnp.int32),
        ],
        compiler_params=pltpu.CompilerParams(vmem_limit_bytes=48 * 2**20),
    )(boxes.reshape(4, regions), shards.reshape(1, regions), wide)

    arrived = pl.pallas_call(
        functools.partial(scatter_kernel, n_row, n_col),
        out_shape=jax.ShapeDtypeStruct((devices, capacity, ch), bf16),
        in_specs=[vmem],
        out_specs=vmem,
        scratch_shapes=[
            pltpu.SemaphoreType.DMA((devices,)),
            pltpu.SemaphoreType.DMA((devices,)),
            pltpu.SemaphoreType.DMA,
        ],
        compiler_params=pltpu.CompilerParams(collective_id=1, has_side_effects=True),
    )(outgoing.reshape(devices, capacity, ch))

    total = devices * capacity
    desc = white_weight.shape[1]
    block = 256
    return pl.pallas_call(
        describe_kernel,
        grid=(total // block,),
        out_shape=jax.ShapeDtypeStruct((total, desc), bf16),
        in_specs=[
            pl.BlockSpec((block, ch), lambda s: (s, 0)),
            pl.BlockSpec((1, ch), lambda s: (0, 0)),
            pl.BlockSpec((ch, desc), lambda s: (0, 0)),
        ],
        out_specs=pl.BlockSpec((block, desc), lambda s: (s, 0)),
        compiler_params=pltpu.CompilerParams(vmem_limit_bytes=32 * 2**20),
    )(arrived.reshape(total, ch), white_mean.reshape(1, ch), white_weight)


def solution(mesh):
    in_specs = (
        P("row", "col", None),
        P(),
        P(),
        P(None, "row", "col", None),
        P("row", "col", None, None),
        P(),
        P(),
    )
    out_specs = P(("row", "col"), None)
    part = functools.partial(body, mesh.shape["row"], mesh.shape["col"])
    return jax.shard_map(part, mesh=mesh, in_specs=in_specs, out_specs=out_specs, check_vma=False)
```

profile of v0, /device:TPU:0, one launch (start us, length us, event | category | flops | bytes accessed | tf_op | source)
XLA Modules:
  0.0 90.0 jit_solution(3880963990478763430)
XLA Ops:
  0.0 1.3 %reshape.24.b = f32[3,1,256]{2,1,0:T(1,128)} reshape(f32[3,256]{1,0:T(4,128)} %param.9) | data formatting | bytes 6144 | tf_op jit(solution)/shard_map/reshape | solution.py:387
  1.3 0.7 copy.10
  2.0 0.0 copy-start.4
  2.0 46.3 %shard_map.73.wide = bf16[32,64,256]{2,1,0:T(8,128)(2,1)} custom-call(bf16[32,128,256]{2,1,0:T(8,128)(2,1)} %feat.1, bf16[3,3,768,256]{3,2,1,0:T(8,128)(2,1)} %bitcast.13, f32[3,1,256]{2,1,0:T(1,128)} %reshape.24.b), custom_call_target="tpu_custom_call" | custom-call | tf_op jit(solution)/shard_map/pallas_call | solution.py:369
  48.2 0.0 copy-done.4
  48.2 0.0 copy-start
  48.3 1.2 %copy-done = bf16[32,64,256]{2,1,0:T(8,128)(2,1)S(1)} copy-done((bf16[32,64,256]{2,1,0:T(8,128)(2,1)S(1)}, bf16[32,64,256]{2,1,0:T(8,128)(2,1)}, u32[]{:S(2)}) %copy-start) | copy-done | bytes 1048600
  49.5 0.0 copy-start.3
  49.5 0.0 copy-start.5
  49.5 12.9 %shard_map.74 = bf16[1024,256]{1,0:T(8,128)(2,1)S(1)} custom-call(s32[4,512]{1,0:T(4,128)S(1)} %bitcast.10, s32[1,512]{1,0:T(1,128)S(1)} %bitcast.11, bf16[32,64,256]{2,1,0:T(8,128)(2,1)S(1)} %copy-done), custom_call_target="tpu_custom_call" | custom-call | tf_op jit(solution)/shard_map/pallas_call | solution.py:391
  62.4 0.0 copy-start.1
  62.4 0.8 copy-done.1
  63.2 22.7 %shard_map.75 = bf16[32,32,256]{2,1,0:T(8,128)(2,1)} custom-call(bf16[32,32,256]{2,1,0:T(8,128)(2,1)} %bitcast.8), custom_call_target="tpu_custom_call" | custom-call | tf_op jit(solution)/shard_map/pallas_call | solution.py:404
  85.9 0.0 copy-done.3
  85.9 0.0 copy-done.5
  85.9 0.0 copy-start.2
  85.9 1.0 %copy-done.2 = bf16[32,32,256]{2,1,0:T(8,128)(2,1)S(1)} copy-done((bf16[32,32,256]{2,1,0:T(8,128)(2,1)S(1)}, bf16[32,32,256]{2,1,0:T(8,128)(2,1)}, u32[]{:S(2)}) %copy-start.2) | copy-done | bytes 524312
  86.9 3.1 %shard_map.76 = bf16[1024,1024]{1,0:T(8,128)(2,1)} custom-call(bf16[1024,256]{1,0:T(8,128)(2,1)S(1)} %bitcast.9, f32[1,256]{1,0:T(1,128)S(1)} %bitcast.12, bf16[256,1024]{1,0:T(8,128)(2,1)S(1)} %copy-done.3), custom_call_target="tpu_custom_call" | custom-call | tf_op jit(solution)/shard_map/pallas_call | solution.py:420
Async XLA Ops:
  2.0 46.3 %copy-start.4 = (s32[1,1,512,1]{2,3,1,0:T(1,128)S(1)}, s32[1,1,512,1]{2,3,1,0:T(1,128)}, u32[]{:S(2)}) copy-start(s32[1,1,512,1]{2,3,1,0:T(1,128)} %param.11) | copy-start | bytes 6148
  48.2 1.2 %copy-start = (bf16[32,64,256]{2,1,0:T(8,128)(2,1)S(1)}, bf16[32,64,256]{2,1,0:T(8,128)(2,1)}, u32[]{:S(2)}) copy-start(bf16[32,64,256]{2,1,0:T(8,128)(2,1)} %shard_map.73.wide) | copy-start | bytes 3145732
  49.5 36.4 %copy-start.3 = (bf16[256,1024]{1,0:T(8,128)(2,1)S(1)}, bf16[256,1024]{1,0:T(8,128)(2,1)}, u32[]{:S(2)}) copy-start(bf16[256,1024]{1,0:T(8,128)(2,1)} %weight.1) | copy-start | bytes 1572868
  49.5 36.4 %copy-start.5 = (f32[256]{0:T(256)S(1)}, f32[256]{0:T(256)}, u32[]{:S(2)}) copy-start(f32[256]{0:T(256)} %param.12) | copy-start | bytes 3076
  62.4 0.8 copy-start.1
  85.9 1.0 %copy-start.2 = (bf16[32,32,256]{2,1,0:T(8,128)(2,1)S(1)}, bf16[32,32,256]{2,1,0:T(8,128)(2,1)}, u32[]{:S(2)}) copy-start(bf16[32,32,256]{2,1,0:T(8,128)(2,1)} %shard_map.75) | copy-start | bytes 1572868
where the time goes:
time: 90.3 us; the launch traced here: 90 us
  Pallas kernels  84.9 us (94%)
  local copies, waits for them, and re-layouts  5.02 us (6%)
    pallas_call x1, Pallas kernels, body(): pl.pallas_call(functools.partial(conv_kernel, n_row, n_col), out_shape=ja...  46.3 us
    pallas_call x1, Pallas kernels, body(): pl.pallas_call(functools.partial(scatter_kernel, n_row, n_col), out_shape...  22.7 us
    pallas_call x1, Pallas kernels, body(): pl.pallas_call(functools.partial(pool_kernel, devices, capacity), out_sha...  12.9 us
    unnamed x13, local copies, waits for them, and re-layouts  3.75 us
    pallas_call x1, Pallas kernels, body(): pl.pallas_call(describe_kernel, grid=(total // block,), out_shape=jax.Sha...  3.08 us

commit v1 on v0

--- a/solution.py
+++ b/solution.py
@@ -13,7 +13,7 @@
 MESH = pl.DeviceIdType.MESH
 
 
-def conv_kernel(n_row, n_col, feat, w, b, wide, a0, xa, xb, xc, load_sem, hs, hr, ms, mr):
+def conv_kernel(n_row, n_col, feat, w, b, wide, a0, xa, xb, xc, red, load_sem, hs, hr, ms, mr):
     rows, cols, ch = feat.shape
     layers = w.shape[0]
     halo = layers
@@ -106,6 +106,8 @@
     def _():
         to_down.start()
 
+    col_at = lax.broadcasted_iota(jnp.int32, (mid_w, ch), 0)
+
     def spread(r):
         x = a0[r].astype(jnp.float32)
         for q in range(3):
@@ -122,13 +124,15 @@
 
     def inner(src, dst, layer, r, count, margin):
         y = taps(src, layer, r, count, mid_w)
-        flat = lax.broadcasted_iota(jnp.int32, (count * mid_w, 1), 0)
-        line = flat // mid_w
-        row_at = r - margin + line
-        col_at = flat - line * mid_w - margin
-        ok = ((row_at >= 0) | (i > 0)) & ((row_at < rows) | (i < n_row - 1))
-        ok = ok & ((col_at >= 0) | (j > 0)) & ((col_at < cols) | (j < n_col - 1))
-        y = jnp.where(ok, y, 0.0)
+        lines = []
+        for k in range(count):
+            row_at = r + k - margin
+            row_ok = ((row_at >= 0) | (i > 0)) & ((row_at < rows) | (i < n_row - 1))
+            low = jnp.where(j > 0, 0, margin)
+            high = jnp.where(row_ok, jnp.where(j < n_col - 1, mid_w, cols + margin), 0)
+            ok = (col_at >= low) & (col_at < high)
+            lines.append(jnp.where(ok, y[k * mid_w:(k + 1) * mid_w], 0.0))
+        y = jnp.concatenate(lines, axis=0)
         for q in range(3):
             moved = y if q == 0 else pltpu.roll(y, count * mid_w - q, 0)
             moved = moved.astype(dst.dtype).reshape(count, mid_w, ch)
@@ -190,8 +194,12 @@
         y = taps(xc, 2, bi * BLK, BLK, cols)
         y = y.reshape(BLK, cols, ch)
         y = jnp.maximum(jnp.maximum(y[0], y[1]), jnp.maximum(y[2], y[3]))
-        y = jnp.max(y.reshape(bcols, BLK, ch), axis=1)
-        wide[i * brows + bi, 0:bcols, :] = y.astype(wide.dtype)
+        halves = []
+        for h in range(ch // 128):
+            red[h, 0:cols, :] = y[:, h * 128:(h + 1) * 128]
+            parts = [red[h, pl.ds(k, bcols, stride=BLK), :] for k in range(BLK)]
+            halves.append(functools.reduce(jnp.maximum, parts))
+        wide[i * brows + bi, 0:bcols, :] = jnp.concatenate(halves, axis=1).astype(wide.dtype)
         for r in range(n_row):
             @pl.when(r != i)
             def _():
@@ -376,6 +384,7 @@
             pltpu.VMEM((rows + 6, mid_w, 3 * ch), bf16),
             pltpu.VMEM((rows + 4, mid_w, 3 * ch), bf16),
             pltpu.VMEM((rows + 2, cols, 3 * ch), bf16),
+            pltpu.VMEM((ch // 128, cols + 8, 128), jnp.float32),
             pltpu.SemaphoreType.DMA,
             pltpu.SemaphoreType.DMA((4,)),
             pltpu.SemaphoreType.DMA((4,)),

time: 90.3 us -> 89.5 us (level)
    pallas_call x1, Pallas kernels: 46.3 us -> 45.2 us  [body(): pl.pallas_call(functools.partial(conv_kernel, n_row, n_col), out_shape=ja...]
where the time goes in v1:
time: 89.5 us; the launch traced here: 89.2 us
  Pallas kernels  84.1 us (94%)
  local copies, waits for them, and re-layouts  5.02 us (6%)
    pallas_call x1, Pallas kernels, body(): pl.pallas_call(functools.partial(conv_kernel, n_row, n_col), out_shape=ja...  45.2 us
    pallas_call x1, Pallas kernels, body(): pl.pallas_call(functools.partial(scatter_kernel, n_row, n_col), out_shape...  22.9 us
    pallas_call x1, Pallas kernels, body(): pl.pallas_call(functools.partial(pool_kernel, devices, capacity), out_sha...  12.9 us
    unnamed x13, local copies, waits for them, and re-layouts  3.75 us
    pallas_call x1, Pallas kernels, body(): pl.pallas_call(describe_kernel, grid=(total // block,), out_shape=jax.Sha...  3.08 us

profile of v1, /device:TPU:0, one launch (start us, length us, event | category | flops | bytes accessed | tf_op | source)
XLA Modules:
  0.0 89.2 jit_solution(17164796182048290618)
XLA Ops:
  0.0 1.3 %reshape.24.b = f32[3,1,256]{2,1,0:T(1,128)} reshape(f32[3,256]{1,0:T(4,128)} %param.9) | data formatting | bytes 6144 | tf_op jit(solution)/shard_map/reshape | solution.py:396
  1.3 0.7 copy.10
  2.0 0.0 copy-start.4
  2.0 45.2 %shard_map.73.wide = bf16[32,64,256]{2,1,0:T(8,128)(2,1)} custom-call(bf16[32,128,256]{2,1,0:T(8,128)(2,1)} %feat.1, bf16[3,3,768,256]{3,2,1,0:T(8,128)(2,1)} %bitcast.13, f32[3,1,256]{2,1,0:T(1,128)} %reshape.24.b), custom_call_target="tpu_custom_call" | custom-call | tf_op jit(solution)/shard_map/pallas_call | solution.py:377
  47.2 0.0 copy-done.4
  47.2 0.0 copy-start
  47.2 1.2 %copy-done = bf16[32,64,256]{2,1,0:T(8,128)(2,1)S(1)} copy-done((bf16[32,64,256]{2,1,0:T(8,128)(2,1)S(1)}, bf16[32,64,256]{2,1,0:T(8,128)(2,1)}, u32[]{:S(2)}) %copy-start) | copy-done | bytes 1048600
  48.4 0.0 copy-start.3
  48.4 0.0 copy-start.5
  48.4 12.9 %shard_map.74 = bf16[1024,256]{1,0:T(8,128)(2,1)S(1)} custom-call(s32[4,512]{1,0:T(4,128)S(1)} %bitcast.10, s32[1,512]{1,0:T(1,128)S(1)} %bitcast.11, bf16[32,64,256]{2,1,0:T(8,128)(2,1)S(1)} %copy-done), custom_call_target="tpu_custom_call" | custom-call | tf_op jit(solution)/shard_map/pallas_call | solution.py:400
  61.3 0.0 copy-start.1
  61.4 0.8 copy-done.1
  62.1 22.9 %shard_map.75 = bf16[32,32,256]{2,1,0:T(8,128)(2,1)} custom-call(bf16[32,32,256]{2,1,0:T(8,128)(2,1)} %bitcast.8), custom_call_target="tpu_custom_call" | custom-call | tf_op jit(solution)/shard_map/pallas_call | solution.py:413
  85.0 0.0 copy-done.3
  85.0 0.0 copy-done.5
  85.0 0.0 copy-start.2
  85.0 1.0 %copy-done.2 = bf16[32,32,256]{2,1,0:T(8,128)(2,1)S(1)} copy-done((bf16[32,32,256]{2,1,0:T(8,128)(2,1)S(1)}, bf16[32,32,256]{2,1,0:T(8,128)(2,1)}, u32[]{:S(2)}) %copy-start.2) | copy-done | bytes 524312
  86.1 3.1 %shard_map.76 = bf16[1024,1024]{1,0:T(8,128)(2,1)} custom-call(bf16[1024,256]{1,0:T(8,128)(2,1)S(1)} %bitcast.9, f32[1,256]{1,0:T(1,128)S(1)} %bitcast.12, bf16[256,1024]{1,0:T(8,128)(2,1)S(1)} %copy-done.3), custom_call_target="tpu_custom_call" | custom-call | tf_op jit(solution)/shard_map/pallas_call | solution.py:429
Async XLA Ops:
  2.0 45.2 %copy-start.4 = (s32[1,1,512,1]{2,3,1,0:T(1,128)S(1)}, s32[1,1,512,1]{2,3,1,0:T(1,128)}, u32[]{:S(2)}) copy-start(s32[1,1,512,1]{2,3,1,0:T(1,128)} %param.11) | copy-start | bytes 6148
  47.2 1.2 %copy-start = (bf16[32,64,256]{2,1,0:T(8,128)(2,1)S(1)}, bf16[32,64,256]{2,1,0:T(8,128)(2,1)}, u32[]{:S(2)}) copy-start(bf16[32,64,256]{2,1,0:T(8,128)(2,1)} %shard_map.73.wide) | copy-start | bytes 3145732
  48.4 36.6 %copy-start.3 = (bf16[256,1024]{1,0:T(8,128)(2,1)S(1)}, bf16[256,1024]{1,0:T(8,128)(2,1)}, u32[]{:S(2)}) copy-start(bf16[256,1024]{1,0:T(8,128)(2,1)} %weight.1) | copy-start | bytes 1572868
  48.4 36.6 %copy-start.5 = (f32[256]{0:T(256)S(1)}, f32[256]{0:T(256)}, u32[]{:S(2)}) copy-start(f32[256]{0:T(256)} %param.12) | copy-start | bytes 3076
  61.3 0.8 copy-start.1
  85.0 1.0 %copy-start.2 = (bf16[32,32,256]{2,1,0:T(8,128)(2,1)S(1)}, bf16[32,32,256]{2,1,0:T(8,128)(2,1)}, u32[]{:S(2)}) copy-start(bf16[32,32,256]{2,1,0:T(8,128)(2,1)} %shard_map.75) | copy-start | bytes 1572868

commit v2 on v1

--- a/solution.py
+++ b/solution.py
@@ -120,7 +120,7 @@
             part = src[pl.ds(r + p, count), 0:width, :].reshape(count * width, 3 * ch)
             prod = jnp.dot(part, w[layer, p], preferred_element_type=jnp.float32)
             acc = prod if acc is None else acc + prod
-        return jnp.maximum(acc + b[layer], 0.0)
+        return jnp.maximum(acc + b[layer:layer + 1, :], 0.0)
 
     def inner(src, dst, layer, r, count, margin):
         y = taps(src, layer, r, count, mid_w)
@@ -226,7 +226,19 @@
                 arrive(bi, 1, r).wait_recv()
 
 
-def pool_kernel(devices, capacity, boxes, shards, wide, out, table, part, lut):
+def pool_kernel(n_row, n_col, boxes, shards, wide, dst, src, table, part, lut,
+                send_sem, recv_sem, own_sem):
+    devices = n_row * n_col
+    capacity = src.shape[1]
+    me = lax.axis_index("row") * n_col + lax.axis_index("col")
+    barrier = pltpu.get_barrier_semaphore()
+
+    @pl.loop(1, devices)
+    def _(k):
+        to = lax.rem(me + k, devices)
+        pl.semaphore_signal(barrier, inc=1, device_id=(to // n_col, lax.rem(to, n_col)),
+                            device_id_type=MESH)
+
     nrow, ncol2, ch = wide.shape
     halves = ch // 128
     regions = shards.shape[1]
@@ -279,10 +291,10 @@
                 got = [jnp.maximum(got[k], got[k + 1]) for k in range(0, len(got), 2)]
             part[h, pl.ds(pl.multiple_of(n * 8, 8), 8), :] = jnp.where(inside, got[0], 0.0)
 
-    @pl.loop(0, regions // 4)
+    @pl.loop(0, regions // 8)
     def _(g):
-        for k in range(4):
-            pool(g * 4 + k)
+        for k in range(8):
+            pool(g * 8 + k)
 
     pooled = jnp.concatenate(
         [
@@ -307,24 +319,12 @@
         pick = (place == target).astype(jnp.float32)
         filled = jnp.sum(pick, axis=1, keepdims=True)
         moved = jnp.dot(pick.astype(jnp.bfloat16), pooled, preferred_element_type=jnp.float32)
-        out[s * size:(s + 1) * size, :] = (moved + (filled - 1.0)).astype(out.dtype)
-
-
-def scatter_kernel(n_row, n_col, src, dst, send_sem, recv_sem, own_sem):
-    devices = n_row * n_col
-    i = lax.axis_index("row")
-    j = lax.axis_index("col")
-    me = i * n_col + j
+        moved = (moved + (filled - 1.0)).astype(src.dtype)
+        group = size // capacity
+        src[s * group:(s + 1) * group] = moved.reshape(group, capacity, ch)
+
     own = pltpu.make_async_copy(src.at[me], dst.at[me], own_sem)
     own.start()
-    barrier = pltpu.get_barrier_semaphore()
-
-    @pl.loop(1, devices)
-    def _(k):
-        to = lax.rem(me + k, devices)
-        pl.semaphore_signal(barrier, inc=1, device_id=(to // n_col, lax.rem(to, n_col)),
-                            device_id_type=MESH)
-
     pl.semaphore_wait(barrier, devices - 1)
 
     def copy(k):
@@ -393,35 +393,27 @@
         ],
         compiler_params=pltpu.CompilerParams(
             collective_id=0, has_side_effects=True, vmem_limit_bytes=56 * 2**20),
-    )(features, conv_weight.reshape(layers, 3, 3 * ch, ch), conv_bias.reshape(layers, 1, ch))
+    )(features, conv_weight.reshape(layers, 3, 3 * ch, ch), conv_bias)
 
     nbr = n_row * brows
     levels = nbr.bit_length()
-    outgoing = pl.pallas_call(
-        functools.partial(pool_kernel, devices, capacity),
-        out_shape=jax.ShapeDtypeStruct((devices * capacity, ch), bf16),
+    arrived = pl.pallas_call(
+        functools.partial(pool_kernel, n_row, n_col),
+        out_shape=jax.ShapeDtypeStruct((devices, capacity, ch), bf16),
         in_specs=[pl.BlockSpec(memory_space=pltpu.SMEM), vmem, vmem],
         out_specs=vmem,
         scratch_shapes=[
+            pltpu.VMEM((devices, capacity, ch), bf16),
             pltpu.VMEM((ch // 128, levels * nbr * 2 * bcols, 128), jnp.float32),
             pltpu.VMEM((ch // 128, regions * 8 + 8, 128), jnp.float32),
             pltpu.SMEM((2, nbr + 1), jnp.int32),
-        ],
-        compiler_params=pltpu.CompilerParams(vmem_limit_bytes=48 * 2**20),
-    )(boxes.reshape(4, regions), shards.reshape(1, regions), wide)
-
-    arrived = pl.pallas_call(
-        functools.partial(scatter_kernel, n_row, n_col),
-        out_shape=jax.ShapeDtypeStruct((devices, capacity, ch), bf16),
-        in_specs=[vmem],
-        out_specs=vmem,
-        scratch_shapes=[
             pltpu.SemaphoreType.DMA((devices,)),
             pltpu.SemaphoreType.DMA((devices,)),
             pltpu.SemaphoreType.DMA,
         ],
-        compiler_params=pltpu.CompilerParams(collective_id=1, has_side_effects=True),
-    )(outgoing.reshape(devices, capacity, ch))
+        compiler_params=pltpu.CompilerParams(
+            collective_id=1, has_side_effects=True, vmem_limit_bytes=48 * 2**20),
+    )(boxes.reshape(4, regions), shards.reshape(1, regions), wide)
 
     total = devices * capacity
     desc = white_weight.shape[1]

time: 89.5 us -> 77.7 us (0.87); the launches traced: 89.2 us -> 76.2 us
  Pallas kernels: 84.1 us -> 74.2 us
  local copies, waits for them, and re-layouts: 5.02 us -> 1.93 us
    pallas_call x2 -> x1, Pallas kernels: 35.8 us -> 25.9 us  [body(): pl.pallas_call(functools.partial(pool_kernel, n_row, n_col), out_shape=ja...]
    unnamed x13 -> x9, local copies, waits for them, and re-layouts: 3.75 us -> 1.93 us
    reshape x1 -> x0, local copies, waits for them, and re-layouts: 1.27 us -> none  [body(): conv_bias.reshape(layers, 1, ch)]
where the time goes in v2:
time: 77.7 us; the launch traced here: 76.2 us
  Pallas kernels  74.2 us (95%)
  local copies, waits for them, and re-layouts  1.93 us (2%)
    pallas_call x1, Pallas kernels, body(): pl.pallas_call(functools.partial(conv_kernel, n_row, n_col), out_shape=ja...  45.3 us
    pallas_call x1, Pallas kernels, body(): pl.pallas_call(functools.partial(pool_kernel, n_row, n_col), out_shape=ja...  25.9 us
    pallas_call x1, Pallas kernels, body(): pl.pallas_call(describe_kernel, grid=(total // block,), out_shape=jax.Sha...  3.11 us
    unnamed x9, local copies, waits for them, and re-layouts  1.93 us

profile of v2, /device:TPU:0, one launch (start us, length us, event | category | flops | bytes accessed | tf_op | source)
XLA Modules:
  0.0 76.2 jit_solution(13668141279433596505)
XLA Ops:
  0.0 0.7 copy.10
  0.7 0.0 copy-start.2
  0.7 0.0 copy-start.1
  0.7 0.0 copy-start.3
  0.7 45.3 %shard_map.73.wide = bf16[32,64,256]{2,1,0:T(8,128)(2,1)} custom-call(bf16[32,128,256]{2,1,0:T(8,128)(2,1)} %feat.1, bf16[3,3,768,256]{3,2,1,0:T(8,128)(2,1)} %bitcast.11, f32[3,256]{1,0:T(4,128)} %b.1), custom_call_target="tpu_custom_call" | custom-call | tf_op jit(solution)/shard_map/pallas_call | solution.py:377
  46.0 0.0 copy-done.2
  46.0 0.0 copy-start
  46.0 1.2 %copy-done = bf16[32,64,256]{2,1,0:T(8,128)(2,1)S(1)} copy-done((bf16[32,64,256]{2,1,0:T(8,128)(2,1)S(1)}, bf16[32,64,256]{2,1,0:T(8,128)(2,1)}, u32[]{:S(2)}) %copy-start) | copy-done | bytes 1048600
  47.2 25.9 %shard_map.74 = bf16[32,32,256]{2,1,0:T(8,128)(2,1)S(1)} custom-call(s32[4,512]{1,0:T(4,128)S(1)} %bitcast.8, s32[1,512]{1,0:T(1,128)S(1)} %bitcast.9, bf16[32,64,256]{2,1,0:T(8,128)(2,1)S(1)} %copy-done), custom_call_target="tpu_custom_call" | custom-call | tf_op jit(solution)/shard_map/pallas_call | solution.py:400
  73.1 0.0 copy-done.1
  73.1 0.0 copy-done.3
  73.1 3.1 %shard_map.75 = bf16[1024,1024]{1,0:T(8,128)(2,1)} custom-call(bf16[1024,256]{1,0:T(8,128)(2,1)S(1)} %bitcast.7, f32[1,256]{1,0:T(1,128)S(1)} %bitcast.10, bf16[256,1024]{1,0:T(8,128)(2,1)S(1)} %copy-done.1), custom_call_target="tpu_custom_call" | custom-call | tf_op jit(solution)/shard_map/pallas_call | solution.py:421
Async XLA Ops:
  0.7 45.3 %copy-start.2 = (s32[1,1,512,1]{2,3,1,0:T(1,128)S(1)}, s32[1,1,512,1]{2,3,1,0:T(1,128)}, u32[]{:S(2)}) copy-start(s32[1,1,512,1]{2,3,1,0:T(1,128)} %param.11) | copy-start | bytes 6148
  0.7 72.4 %copy-start.1 = (bf16[256,1024]{1,0:T(8,128)(2,1)S(1)}, bf16[256,1024]{1,0:T(8,128)(2,1)}, u32[]{:S(2)}) copy-start(bf16[256,1024]{1,0:T(8,128)(2,1)} %weight.1) | copy-start | bytes 1572868
  0.7 72.4 %copy-start.3 = (f32[256]{0:T(256)S(1)}, f32[256]{0:T(256)}, u32[]{:S(2)}) copy-start(f32[256]{0:T(256)} %param.12) | copy-start | bytes 3076
  46.0 1.2 %copy-start = (bf16[32,64,256]{2,1,0:T(8,128)(2,1)S(1)}, bf16[32,64,256]{2,1,0:T(8,128)(2,1)}, u32[]{:S(2)}) copy-start(bf16[32,64,256]{2,1,0:T(8,128)(2,1)} %shard_map.73.wide) | copy-start | bytes 3145732

commit v3 on v2

--- a/solution.py
+++ b/solution.py
@@ -138,12 +138,13 @@
             moved = moved.astype(dst.dtype).reshape(count, mid_w, ch)
             dst[pl.ds(r, count), :, q * ch:(q + 1) * ch] = moved[:, :dst.shape[1]]
 
-    @pl.loop(halo, halo + rows)
-    def _(r):
-        spread(r)
+    @pl.loop(0, rows // 4)
+    def _(g):
+        for k in range(4):
+            spread(halo + g * 4 + k)
 
     first = halo
-    count1 = 3
+    count1 = 6
     steps1 = (rows - 2) // count1
 
     @pl.loop(0, steps1)
@@ -167,7 +168,7 @@
 
     @pl.loop(0, 2)
     def _(s):
-        inner(xa, xb, 0, s * (rows + 1), count1, 2)
+        inner(xa, xb, 0, s * (rows + 1), halo, 2)
 
     @pl.loop(0, (rows + 2) // 4)
     def _(s):

time: 77.7 us -> 77.7 us (level)
  no operation moved by 1% of the time
where the time goes in v3:
time: 77.7 us; the launch traced here: 76.2 us
  Pallas kernels  74.2 us (95%)
  local copies, waits for them, and re-layouts  1.93 us (2%)
    pallas_call x1, Pallas kernels, body(): pl.pallas_call(functools.partial(conv_kernel, n_row, n_col), out_shape=ja...  45.3 us
    pallas_call x1, Pallas kernels, body(): pl.pallas_call(functools.partial(pool_kernel, n_row, n_col), out_shape=ja...  25.9 us
    pallas_call x1, Pallas kernels, body(): pl.pallas_call(describe_kernel, grid=(total // block,), out_shape=jax.Sha...  3.11 us
    unnamed x9, local copies, waits for them, and re-layouts  1.93 us

profile of v3, /device:TPU:0, one launch (start us, length us, event | category | flops | bytes accessed | tf_op | source)
XLA Modules:
  0.0 76.2 jit_solution(3394488741999869441)
XLA Ops:
  0.0 0.7 copy.10
  0.7 0.0 copy-start.2
  0.7 0.0 copy-start.1
  0.7 0.0 copy-start.3
  0.7 45.3 %shard_map.73.wide = bf16[32,64,256]{2,1,0:T(8,128)(2,1)} custom-call(bf16[32,128,256]{2,1,0:T(8,128)(2,1)} %feat.1, bf16[3,3,768,256]{3,2,1,0:T(8,128)(2,1)} %bitcast.11, f32[3,256]{1,0:T(4,128)} %b.1), custom_call_target="tpu_custom_call" | custom-call | tf_op jit(solution)/shard_map/pallas_call | solution.py:378
  46.0 0.0 copy-done.2
  46.0 0.0 copy-start
  46.0 1.2 %copy-done = bf16[32,64,256]{2,1,0:T(8,128)(2,1)S(1)} copy-done((bf16[32,64,256]{2,1,0:T(8,128)(2,1)S(1)}, bf16[32,64,256]{2,1,0:T(8,128)(2,1)}, u32[]{:S(2)}) %copy-start) | copy-done | bytes 1048600
  47.2 25.9 %shard_map.74 = bf16[32,32,256]{2,1,0:T(8,128)(2,1)S(1)} custom-call(s32[4,512]{1,0:T(4,128)S(1)} %bitcast.8, s32[1,512]{1,0:T(1,128)S(1)} %bitcast.9, bf16[32,64,256]{2,1,0:T(8,128)(2,1)S(1)} %copy-done), custom_call_target="tpu_custom_call" | custom-call | tf_op jit(solution)/shard_map/pallas_call | solution.py:401
  73.1 0.0 copy-done.1
  73.1 0.0 copy-done.3
  73.1 3.1 %shard_map.75 = bf16[1024,1024]{1,0:T(8,128)(2,1)} custom-call(bf16[1024,256]{1,0:T(8,128)(2,1)S(1)} %bitcast.7, f32[1,256]{1,0:T(1,128)S(1)} %bitcast.10, bf16[256,1024]{1,0:T(8,128)(2,1)S(1)} %copy-done.1), custom_call_target="tpu_custom_call" | custom-call | tf_op jit(solution)/shard_map/pallas_call | solution.py:422
Async XLA Ops:
  0.7 45.3 %copy-start.2 = (s32[1,1,512,1]{2,3,1,0:T(1,128)S(1)}, s32[1,1,512,1]{2,3,1,0:T(1,128)}, u32[]{:S(2)}) copy-start(s32[1,1,512,1]{2,3,1,0:T(1,128)} %param.11) | copy-start | bytes 6148
  0.7 72.4 %copy-start.1 = (bf16[256,1024]{1,0:T(8,128)(2,1)S(1)}, bf16[256,1024]{1,0:T(8,128)(2,1)}, u32[]{:S(2)}) copy-start(bf16[256,1024]{1,0:T(8,128)(2,1)} %weight.1) | copy-start | bytes 1572868
  0.7 72.4 %copy-start.3 = (f32[256]{0:T(256)S(1)}, f32[256]{0:T(256)}, u32[]{:S(2)}) copy-start(f32[256]{0:T(256)} %param.12) | copy-start | bytes 3076
  46.0 1.2 %copy-start = (bf16[32,64,256]{2,1,0:T(8,128)(2,1)S(1)}, bf16[32,64,256]{2,1,0:T(8,128)(2,1)}, u32[]{:S(2)}) copy-start(bf16[32,64,256]{2,1,0:T(8,128)(2,1)} %shard_map.73.wide) | copy-start | bytes 3145732
